TPU v7x, 32 devices: a whole 2x2x4 slice. The times are simulated.
32 devices in a mesh: groups: 2 (over y), seq: 4 (over x, core), tensor: 4 (over z).
Axes of the slice: x: 2, y: 2, z: 4, core: 2. Of those that a mesh axis runs over, the one named last changes fastest.
Arguments:
- spectrum: bfloat16 [12288, 80], P(('groups', 'seq')), parts along dimension 0, may hold values from -6 to 6
- conv_weight: bfloat16 [3, 80, 1536], P(None, None, 'tensor'), may hold values from -0.375 to 0.375
- conv_bias: float32 [1536], P('tensor'), may hold values from -3 to 3
- depth_weight: float32 [3, 1536], replicated, may hold values from -3 to 3
- depth_bias: float32 [1536], replicated, may hold values from -3 to 3
- mix_gain: float32 [1536], replicated, may hold values from 0.5 to 1.5
- mix_shift: float32 [1536], replicated, may hold values from -3 to 3
- feed_gain: float32 [1536], replicated, may hold values from 0.5 to 1.5
- feed_shift: float32 [1536], replicated, may hold values from -3 to 3
- heads_weight: bfloat16 [1536, 4608], P(None, 'tensor'), may hold values from -0.15625 to 0.15625
- heads_bias: float32 [4608], P('tensor'), may hold values from -3 to 3
- up_weight: bfloat16 [1536, 6144], P(None, 'tensor'), may hold values from -0.15625 to 0.15625
- up_bias: float32 [6144], P('tensor'), may hold values from -3 to 3
Outputs:
- attention_inputs: bfloat16 [3072, 4608], P(('groups', 'seq'), 'tensor'), parts along dimension 0
- feed_hidden: bfloat16 [3072, 6144], P(('groups', 'seq'), 'tensor'), parts along dimension 0
There are 2 independent parts, one for each index of `groups`. A program takes and returns all parts, laid end to end along the dimension named above; an argument that names none is the same for every part. Nothing has to cross between parts.
All inputs are finite; a program needn't handle non-finite values.
Results may differ from a plain program's by a relative error of at most 0.009.
Values may be sent and summed in bfloat16 or wider, within the bound.
A program may use at most 128 MiB of HBM per device.

v0:
```python
import jax
import jax.numpy as jnp
from jax import lax
from jax.sharding import PartitionSpec as P

epsilon = 1e-05


def passed_along(value, axis, steps):
    count = lax.axis_size(axis)
    initial, last = (max(0, -steps), min(count, count - steps))
    return lax.ppermute(value, axis, [(source, source + steps) for source in range(initial, last)])


def conv_rows(prior_rows, even_rows, odd_rows, conv_weight, conv_bias):
    stacked = jnp.concatenate([prior_rows, even_rows, odd_rows], axis=1)
    flat_weight = conv_weight.reshape(-1, conv_weight.shape[2])
    summed = jnp.dot(stacked, flat_weight, preferred_element_type=jnp.float32) + conv_bias
    return jax.nn.relu(summed).astype(jnp.bfloat16)


def first_conv(spectrum, prior_row, conv_weight, conv_bias):
    even_rows = spectrum[0::2]
    odd_rows = spectrum[1::2]
    prior_rows = jnp.concatenate([prior_row, odd_rows[:-1]], axis=0)
    return conv_rows(prior_rows, even_rows, odd_rows, conv_weight, conv_bias)


def depth_conv(channels, prior_row, depth_weight, depth_bias):
    even_half = channels[0::2].astype(jnp.float32)
    odd_half = channels[1::2].astype(jnp.float32)
    prior_half = jnp.concatenate([prior_row.astype(jnp.float32), odd_half[:-1]], axis=0)
    summed = (
        prior_half * depth_weight[0]
        + even_half * depth_weight[1]
        + odd_half * depth_weight[2]
        + depth_bias
    )
    return jax.nn.relu(summed).astype(jnp.bfloat16)


def channel_depth(channels, own_weight, own_bias):
    prior_row = passed_along(channels[-1:], "seq", 1)
    return depth_conv(channels, prior_row, own_weight, own_bias)


def per_device(
    spectrum,
    conv_weight,
    conv_bias,
    depth_weight,
    depth_bias,
    mix_gain,
    mix_shift,
    feed_gain,
    feed_shift,
    heads_weight,
    heads_bias,
    up_weight,
    up_bias,
):
    mel_prior = passed_along(spectrum[-1:], "seq", 1)
    channels = first_conv(spectrum, mel_prior, conv_weight, conv_bias)
    own_width = channels.shape[1]
    lane_index = lax.axis_index("tensor")
    own_weight = lax.dynamic_slice_in_dim(depth_weight, lane_index * own_width, own_width, 1)
    own_bias = lax.dynamic_slice_in_dim(depth_bias, lane_index * own_width, own_width, 0)
    reduced = channel_depth(channels, own_weight, own_bias)
    subsampled = lax.all_to_all(reduced, "tensor", split_axis=0, concat_axis=1, tiled=True)
    frames_float = lax.all_gather(subsampled, "tensor", axis=0, tiled=True).astype(jnp.float32)
    row_mean = jnp.mean(frames_float, axis=-1, keepdims=True)
    centred = frames_float - row_mean
    variance = jnp.mean(centred * centred, axis=-1, keepdims=True)
    normed = centred * lax.rsqrt(variance + epsilon)
    mix_input = (normed * mix_gain + mix_shift).astype(jnp.bfloat16)
    feed_input = (normed * feed_gain + feed_shift).astype(jnp.bfloat16)
    heads_out = (
        jnp.dot(mix_input, heads_weight, preferred_element_type=jnp.float32) + heads_bias
    ).astype(jnp.bfloat16)
    raised = jnp.dot(feed_input, up_weight, preferred_element_type=jnp.float32) + up_bias
    gated = jax.nn.silu(raised).astype(jnp.bfloat16)
    projected = jnp.concatenate([heads_out, gated], axis=1)
    heads_cols = heads_weight.shape[1]
    return (projected[:, :heads_cols], projected[:, heads_cols:])


def solution(mesh):
    in_specs = (
        P(("groups", "seq"), None),
        P(None, None, "tensor"),
        P("tensor"),
        P(),
        P(),
        P(),
        P(),
        P(),
        P(),
        P(None, "tensor"),
        P("tensor"),
        P(None, "tensor"),
        P("tensor"),
    )
    out_specs = (P(("groups", "seq"), "tensor"), P(("groups", "seq"), "tensor"))
    return jax.shard_map(
        per_device, mesh=mesh, in_specs=in_specs, out_specs=out_specs, check_vma=False
    )
```

profile of v0, /device:TPU:0, one launch (start us, length us, event | category | flops | bytes accessed | tf_op | source)
XLA Modules:
  0.0 102.4 jit_solution(2732610527631053864)
XLA Ops:
  7.2 0.0 copy-start
  7.2 0.0 all-gather.2.cloned.1.call-start
  7.2 1.6 %slice.33 = bf16[1,80]{0,1:T(8,128)(2,1)} slice(bf16[1536,80]{0,1:T(8,128)(2,1)} %param.13), slice={[1535:1536], [0:80]} | slice | bytes 320 | tf_op jit(solution)/shard_map/slice | solution.py:62
  8.8 3.0 %collective-permute-start = (bf16[1,80]{0,1:T(8,128)(2,1)}, bf16[1,80]{0,1:T(8,128)(2,1)}, u32[]{:S(2)}, u32[]{:S(2)}) collective-permute-start(bf16[1,80]{0,1:T(8,128)(2,1)} %slice.33), channel_id=1, source_target_pairs={{0,4},{4,8},{8,12},{1,5},{5,9},{9,13},{2,6},{6,10},{10,14},{3,7},{... | collective-permute-start | bytes 488 | tf_op jit(solution)/shard_map/ppermute | solution.py:12
  11.7 5.7 %slice.34 = bf16[768,80]{0,1:T(8,128)(2,1)} slice(bf16[1536,80]{0,1:T(8,128)(2,1)} %param.13), slice={[1:1536:2], [0:80:1]} | slice | bytes 245760 | tf_op jit(solution)/shard_map/slice | solution.py:24
  17.5 5.7 %slice.36 = bf16[768,80]{0,1:T(8,128)(2,1)} slice(bf16[1536,80]{0,1:T(8,128)(2,1)} %param.13), slice={[0:1536:2], [0:80:1]} | slice | bytes 245760 | tf_op jit(solution)/shard_map/slice | solution.py:23
  23.2 1.7 %fusion.11 = bf16[768,384]{1,0:T(8,128)(2,1)S(1)} fusion(bf16[240,384]{1,0:T(8,128)(2,1)} %bitcast.15, f32[384]{0:T(512)} %param.15, bf16[768,80]{0,1:T(8,128)(2,1)} %slice.34, bf16[768,80]{0,1:T(8,128)(2,1)} %slice.36, bf16[767,80]{0,1:T(8,128)(2,1)} %bitcast.12, bf16[1,80]{0,1:T(8,128)(2,1)} %collective-permute-done), kind=kOutput, calls=%fused_computation.17 | convolution fusion | flops 143917056 | bytes 1144320 | tf_op jit(solution)/shard_map/dot_general | solution.py:18
  24.9 0.0 copy-start.2
  24.9 0.8 copy-done.2
  25.7 0.5 slice.45
  26.3 4.5 %collective-permute-start.1 = (bf16[1,384]{1,0:T(2,128)(2,1)}, bf16[1,384]{1,0:T(2,128)(2,1)}, u32[]{:S(2)}, u32[]{:S(2)}) collective-permute-start(bf16[1,384]{1,0:T(2,128)(2,1)} %slice.45), channel_id=1, source_target_pairs={{0,4},{4,8},{8,12},{1,5},{5,9},{9,13},{2,6},{6,10},{10,14},{3,7},{... | collective-permute-start | bytes 2312 | tf_op jit(solution)/shard_map/ppermute | solution.py:12
  30.7 0.8 dynamic_slice.7
  31.5 0.9 dynamic-slice_reduce_fusion.2
  32.4 3.6 %slice.38 = bf16[384,384]{1,0:T(8,128)(2,1)} slice(bf16[768,384]{1,0:T(8,128)(2,1)} %copy-done.2), slice={[1:768:2], [0:384:1]} | slice | bytes 589824 | tf_op jit(solution)/shard_map/slice | solution.py:31
  36.0 3.6 %slice.41 = bf16[384,384]{1,0:T(8,128)(2,1)} slice(bf16[768,384]{1,0:T(8,128)(2,1)} %copy-done.2), slice={[0:768:2], [0:384:1]} | slice | bytes 589824 | tf_op jit(solution)/shard_map/slice | solution.py:30
  39.6 1.0 slice.46
  40.6 0.7 convert_element_type.31
  41.2 1.3 %fusion.26 = bf16[384,384]{1,0:T(8,128)(2,1)S(1)} fusion(f32[383,384]{1,0:T(8,128)S(1)} %slice.46, f32[1,384]{1,0:T(1,128)S(1)} %convert_element_type.31, bf16[384,384]{1,0:T(8,128)(2,1)} %slice.41, f32[384]{0:T(512)S(1)} %dynamic_slice.7, f32[384]{0:T(512)S(1)} %get-tuple-element.4, f32[384]{0:T(512)S(1)} %get-tuple-element.3, f32[384]{0:T(512)S(1)} %get-tuple-element.2, ...), kind=kLoop, calls=%fused_computation.31 | loop fusion | flops 1622016 | bytes 1480704 | tf_op jit(solution)/shard_map/convert_element_type | solution.py:39
  42.5 0.0 copy-start.3
  42.5 0.0 copy-start.4
  42.6 13.9 %all_to_all.19 = bf16[4,96,384]{2,1,0:T(8,128)(2,1)S(1)} all-to-all(bf16[4,96,384]{2,1,0:T(8,128)(2,1)S(1)} %bitcast.11), channel_id=1, replica_groups=mesh['groups'=2,'seq'=4,'tensor'=4] {'tensor'}, dimensions={0} | all-to-all | bytes 589824 | tf_op jit(solution)/shard_map/all_to_all | solution.py:69
  56.4 0.7 copy.17
  57.2 0.0 all-gather.2.cloned.1.call-update
  57.2 28.8 %all-gather.2.cloned.1.call-done = bf16[384,1536]{1,0:T(8,128)(2,1)} async-done(((bf16[96,1536]{1,0:T(8,128)(2,1)}), bf16[384,1536]{1,0:T(8,128)(2,1)}) %all-gather.2.cloned.1.call-update) | async-done | bytes 1179664 | tf_op jit(solution)/shard_map/all_gather | solution.py:70
  86.0 1.6 %convert_reduce_fusion = f32[384]{0:T(512)S(1)} fusion(bf16[384,1536]{1,0:T(8,128)(2,1)} %all-gather.2.cloned.1.call-done), kind=kLoop, calls=%fused_computation.3 | loop fusion | flops 1179264 | bytes 1181184 | tf_op jit(solution)/shard_map/reduce_sum | solution.py:71
  87.6 1.9 %fusion.9 = f32[384]{0:T(512)S(1)} fusion(bf16[384,1536]{1,0:T(8,128)(2,1)} %all-gather.2.cloned.1.call-done, f32[384]{0:T(512)S(1)} %broadcast_multiply_fusion), kind=kLoop, calls=%fused_computation.13 | loop fusion | flops 2358912 | bytes 1182720 | tf_op jit(solution)/shard_map/reduce_sum | solution.py:73
  89.5 0.0 slice-start.1
  89.5 0.0 copy-start.6
  89.5 0.0 copy-start.7
  89.6 0.0 copy-start.8
  89.6 2.7 %fusion.2 = bf16[384,1152]{1,0:T(8,128)(2,1)} fusion(bf16[1536,1152]{1,0:T(8,128)(2,1)S(1)} %copy-done, bf16[384,1536]{1,0:T(8,128)(2,1)S(1)} %copy-done.1, f32[1536]{0:T(1024)S(1)} %copy-done.3, f32[1536]{0:T(1024)S(1)} %copy-done.4, f32[384]{0:T(512)S(1)} %add_rsqrt_fusion, f32[384]{0:T(512)S(1)} %broadcast_multiply_fusion, f32[1152]{0:T(1024)S(1)} %copy-done.5), kind=kOutput, calls=%fused_computation.6 | convolution fusion | flops 1363378176 | bytes 5623296 | tf_op jit(solution)/shard_map/dot_general | solution.py:78
  92.3 3.3 %multiply_convert_fusion = bf16[384,1536]{1,0:T(8,128)(2,1)} fusion(bf16[1536,1536]{1,0:T(8,128)(2,1)S(1)} %bitcast.14, bf16[384,1536]{1,0:T(8,128)(2,1)S(1)} %copy-done.1, f32[1536]{0:T(1024)S(1)} %copy-done.6, f32[1536]{0:T(1024)S(1)} %copy-done.7, f32[1536]{0:T(1024)S(1)} %copy-done.8, f32[384]{0:T(512)S(1)} %add_rsqrt_fusion, ...), kind=kOutput, calls=%fused_computation.14 | convolution fusion | flops 1819017216 | bytes 7099392 | tf_op jit(solution)/shard_map/dot_general | solution.py:80
  (18 shorter events, 0.0 us)
Async XLA Ops:
  7.2 82.3 %copy-start = (bf16[1536,1152]{1,0:T(8,128)(2,1)S(1)}, bf16[1536,1152]{1,0:T(8,128)(2,1)}, u32[]{:S(2)}) copy-start(bf16[1536,1152]{1,0:T(8,128)(2,1)} %param.22) | copy-start | bytes 10616836
  7.2 78.8 %all-gather.2.cloned.1.call-start = ((), (), s32[]{:S(2)}) async-start(), calls=%async_computation.1 | async-start | bytes 1474560 | tf_op jit(solution)/shard_map/all_gather | solution.py:70
  8.8 14.4 %collective-permute-start = (bf16[1,80]{0,1:T(8,128)(2,1)}, bf16[1,80]{0,1:T(8,128)(2,1)}, u32[]{:S(2)}, u32[]{:S(2)}) collective-permute-start(bf16[1,80]{0,1:T(8,128)(2,1)} %slice.33), channel_id=1, source_target_pairs={{0,4},{4,8},{8,12},{1,5},{5,9},{9,13},{2,6},{6,10},{10,14},{3,7},{... | collective-permute-start | bytes 488 | tf_op jit(solution)/shard_map/ppermute | solution.py:12
  24.9 0.8 copy-start.2
  26.3 14.3 %collective-permute-start.1 = (bf16[1,384]{1,0:T(2,128)(2,1)}, bf16[1,384]{1,0:T(2,128)(2,1)}, u32[]{:S(2)}, u32[]{:S(2)}) collective-permute-start(bf16[1,384]{1,0:T(2,128)(2,1)} %slice.45), channel_id=1, source_target_pairs={{0,4},{4,8},{8,12},{1,5},{5,9},{9,13},{2,6},{6,10},{10,14},{3,7},{... | collective-permute-start | bytes 2312 | tf_op jit(solution)/shard_map/ppermute | solution.py:12
  42.5 46.9 %copy-start.3 = (f32[1536]{0:T(1024)S(1)}, f32[1536]{0:T(1024)}, u32[]{:S(2)}) copy-start(f32[1536]{0:T(1024)} %param.19) | copy-start | bytes 18436
  42.5 46.9 %copy-start.4 = (f32[1536]{0:T(1024)S(1)}, f32[1536]{0:T(1024)}, u32[]{:S(2)}) copy-start(f32[1536]{0:T(1024)} %param.18) | copy-start | bytes 18436
  86.0 3.5 %copy-start.1 = (bf16[384,1536]{1,0:T(8,128)(2,1)S(1)}, bf16[384,1536]{1,0:T(8,128)(2,1)}, u32[]{:S(2)}) copy-start(bf16[384,1536]{1,0:T(8,128)(2,1)} %all-gather.2.cloned.1.call-done) | copy-start | bytes 3538948
  86.0 3.5 %copy-start.5 = (f32[1152]{0:T(1024)S(1)}, f32[1152]{0:T(1024)}, u32[]{:S(2)}) copy-start(f32[1152]{0:T(1024)} %param.23) | copy-start | bytes 13828
  87.6 4.7 %slice-start = ((s8[4718592]{0:T(1024)(128)(4,1)}), s8[4194304]{0:T(1024)(128)(4,1)S(1)}, s32[]{:S(2)}) async-start(s8[4718592]{0:T(1024)(128)(4,1)} %bitcast.13), calls=%async_computation.2 | async-start | bytes 8388608
  89.5 2.7 %slice-start.1 = ((s8[4718592]{0:T(1024)(128)(4,1)}), s8[524288]{0:T(1024)(128)(4,1)S(1)}, s32[]{:S(2)}) async-start(s8[4718592]{0:T(1024)(128)(4,1)} %bitcast.13), calls=%async_computation.3 | async-start | bytes 1048576
  89.5 2.7 %copy-start.6 = (f32[1536]{0:T(1024)S(1)}, f32[1536]{0:T(1024)}, u32[]{:S(2)}) copy-start(f32[1536]{0:T(1024)} %param.25) | copy-start | bytes 18436
  89.5 2.7 %copy-start.7 = (f32[1536]{0:T(1024)S(1)}, f32[1536]{0:T(1024)}, u32[]{:S(2)}) copy-start(f32[1536]{0:T(1024)} %param.21) | copy-start | bytes 18436
  89.6 2.7 %copy-start.8 = (f32[1536]{0:T(1024)S(1)}, f32[1536]{0:T(1024)}, u32[]{:S(2)}) copy-start(f32[1536]{0:T(1024)} %param.20) | copy-start | bytes 18436
Sparse Core Ops, SparseCore 0:
  57.3 28.6 all-gather.1
where the time goes:
time: 103 us; the launch traced here: 102 us
  waiting for transfers between devices  28.8 us (28%)
  local copies, waits for them, and re-layouts  25 us (24%)
  between operations  14.2 us (14%)
  blocking collectives  13.9 us (13%)
  matrix products  7.7 us (7%)
  starting transfers between devices  7.47 us (7%)
  other arithmetic  5.43 us (5%)
    all_gather x1, waiting for transfers between devices, per_device(): lax.all_gather(subsampled, 'tensor', axis=0, tiled=True).astype(jnp.float32)  28.8 us
    all_to_all x1, blocking collectives, per_device(): lax.all_to_all(reduced, 'tensor', split_axis=0, concat_axis=1, tiled=True)  13.9 us
    ppermute x2, starting transfers between devices, passed_along(): lax.ppermute(value, axis, [(source, source + steps) for source in range(i...  7.44 us
    slice x1, local copies, waits for them, and re-layouts, first_conv(): odd_rows = spectrum[1::2]  5.72 us
    slice x1, local copies, waits for them, and re-layouts, first_conv(): even_rows = spectrum[0::2]  5.72 us
    slice x1, local copies, waits for them, and re-layouts, depth_conv(): odd_half = channels[1::2].astype(jnp.float32)  3.58 us
    slice x1, local copies, waits for them, and re-layouts, depth_conv(): even_half = channels[0::2].astype(jnp.float32)  3.57 us
    dot_general x1, matrix products, per_device(): jnp.dot(feed_input, up_weight, preferred_element_type=jnp.float32) + up_bias  3.31 us
  transfers between devices with their start and end apart: 3, of which 1 were waited for; matrix products, arithmetic and copies ran while one was open for 21% of the time, Pallas kernels for 0%

commit v1 on v0

--- a/solution.py
+++ b/solution.py
@@ -1,9 +1,15 @@
+import functools
+
 import jax
 import jax.numpy as jnp
 from jax import lax
+from jax.experimental import pallas as pl
+from jax.experimental.pallas import tpu as pltpu
 from jax.sharding import PartitionSpec as P
 
 epsilon = 1e-05
+HALO = 16
+MESH = pl.DeviceIdType.MESH
 
 
 def passed_along(value, axis, steps):
@@ -39,12 +45,7 @@
     return jax.nn.relu(summed).astype(jnp.bfloat16)
 
 
-def channel_depth(channels, own_weight, own_bias):
-    prior_row = passed_along(channels[-1:], "seq", 1)
-    return depth_conv(channels, prior_row, own_weight, own_bias)
-
-
-def per_device(
+def plain_device(
     spectrum,
     conv_weight,
     conv_bias,
@@ -65,7 +66,8 @@
     lane_index = lax.axis_index("tensor")
     own_weight = lax.dynamic_slice_in_dim(depth_weight, lane_index * own_width, own_width, 1)
     own_bias = lax.dynamic_slice_in_dim(depth_bias, lane_index * own_width, own_width, 0)
-    reduced = channel_depth(channels, own_weight, own_bias)
+    prior_row = passed_along(channels[-1:], "seq", 1)
+    reduced = depth_conv(channels, prior_row, own_weight, own_bias)
     subsampled = lax.all_to_all(reduced, "tensor", split_axis=0, concat_axis=1, tiled=True)
     frames_float = lax.all_gather(subsampled, "tensor", axis=0, tiled=True).astype(jnp.float32)
     row_mean = jnp.mean(frames_float, axis=-1, keepdims=True)
@@ -79,9 +81,332 @@
     ).astype(jnp.bfloat16)
     raised = jnp.dot(feed_input, up_weight, preferred_element_type=jnp.float32) + up_bias
     gated = jax.nn.silu(raised).astype(jnp.bfloat16)
-    projected = jnp.concatenate([heads_out, gated], axis=1)
-    heads_cols = heads_weight.shape[1]
-    return (projected[:, :heads_cols], projected[:, heads_cols:])
+    return heads_out, gated
+
+
+def tiles_of(width, tile):
+    whole = width // tile
+    return whole, width - whole * tile
+
+
+def front_kernel(
+    count,
+    mels,
+    spectrum,
+    conv_weight,
+    conv_bias,
+    depth_weight,
+    depth_bias,
+    mix_gain,
+    mix_shift,
+    feed_gain,
+    feed_shift,
+    heads_bias,
+    up_bias,
+    heads_hbm,
+    up_hbm,
+    heads_out,
+    up_out,
+    heads_w,
+    up_w,
+    gathered,
+    halo,
+    frames,
+    stacked,
+    subsampled,
+    mix_input,
+    feed_input,
+    heads_stage,
+    up_stage,
+    load_sem,
+    halo_sem,
+    send1,
+    recv1,
+    send2,
+    recv2,
+    send3,
+    recv3,
+    heads_sem,
+    up_sem,
+):
+    group = lax.axis_index("groups")
+    span = lax.axis_index("seq")
+    lane = lax.axis_index("tensor")
+    taps, width = conv_weight.shape
+    depth = gathered.shape[1]
+    piece_rows = depth // 8
+    rows = subsampled.shape[0]
+    mel_rows = spectrum.shape[0]
+    channels = subsampled.shape[1]
+
+    core = lax.rem(span, 2)
+    sibling = span + 1 - 2 * core
+    across = lax.rem(span + 2, 4)
+    other = 1 - group
+    following = lax.rem(span + 1, 4)
+
+    load_heads = pltpu.make_async_copy(heads_hbm, heads_w, load_sem.at[0])
+    load_up = pltpu.make_async_copy(up_hbm, up_w, load_sem.at[1])
+
+    barrier = pltpu.get_barrier_semaphore()
+    peers = [(group, span, lax.rem(lane + k, count)) for k in range(1, count)]
+    peers += [(group, sibling, lane), (group, across, lane), (group, 3 - span, lane)]
+    peers += [(other, span, lane), (other, across, lane)]
+    for peer in peers:
+        pl.semaphore_signal(barrier, inc=1, device_id=peer, device_id_type=MESH)
+
+    gathered[lane, 0:taps, :] = conv_weight[...]
+    bias = conv_bias[...]
+    high = bias.astype(jnp.bfloat16).astype(jnp.float32)
+    row_id = lax.broadcasted_iota(jnp.int32, (depth - taps, width), 0)
+    bias_rows = jnp.where(row_id == 0, high, jnp.where(row_id == 1, bias - high, 0.0))
+    gathered[lane, taps:depth, :] = bias_rows.astype(jnp.bfloat16)
+
+    pl.semaphore_wait(barrier, len(peers))
+
+    def piece(shard, owner_group, owner_span):
+        start = pl.multiple_of((owner_group * 4 + owner_span) * piece_rows, piece_rows)
+        return gathered.at[shard, pl.ds(start, piece_rows), :]
+
+    def send(part, target, send_sem, recv_sem):
+        return pltpu.make_async_remote_copy(
+            src_ref=part,
+            dst_ref=part,
+            send_sem=send_sem,
+            recv_sem=recv_sem,
+            device_id=target,
+            device_id_type=MESH,
+        )
+
+    sources = [lax.rem(lane + count - k, count) for k in range(1, count)]
+    first = []
+    for k in range(1, count):
+        copy = send(
+            piece(lane, group, span),
+            (group, span, lax.rem(lane + k, count)),
+            send1.at[k - 1],
+            recv1.at[k - 1],
+        )
+        copy.start()
+        first.append(copy)
+    halo_copy = pltpu.make_async_remote_copy(
+        src_ref=spectrum.at[pl.ds(mel_rows - HALO, HALO), :],
+        dst_ref=halo,
+        send_sem=halo_sem.at[0],
+        recv_sem=halo_sem.at[1],
+        device_id=(group, following, lane),
+        device_id_type=MESH,
+    )
+    halo_copy.start()
+    load_heads.start()
+    load_up.start()
+
+    frames[HALO : HALO + mel_rows, 0:mels] = spectrum[...].astype(jnp.float32)
+
+    chips = [(group, across), (other, span), (other, across)]
+    second = []
+    for k in range(count - 1):
+        first[k].wait_recv()
+        part = piece(sources[k], group, span)
+        copies = []
+        for j, (to_group, to_span) in enumerate(chips):
+            copies.append(send(part, (to_group, to_span, lane), send2.at[k, j], recv2.at[k, j]))
+        copies.append(send(part, (group, sibling, lane), send2.at[k, 3], recv2.at[k, 3]))
+        for copy in copies:
+            copy.start()
+        second.append(copies)
+
+    halo_copy.wait_recv()
+    frames[0:HALO, 0:mels] = jnp.where(span == 0, 0.0, halo[...].astype(jnp.float32))
+
+    def tap(offset):
+        return frames[pl.ds(HALO + offset, rows, stride=4), :][:, 0:mels]
+
+    taken = {offset: tap(offset) for offset in range(-3, 4)}
+    tail_id = lax.broadcasted_iota(jnp.int32, (rows, depth - taps), 1)
+    tail = jnp.where(tail_id < 2, 1.0, 0.0)
+    row_zero = lax.broadcasted_iota(jnp.int32, (rows, depth - taps), 0) == 0
+    start_tail = jnp.where(row_zero & (span == 0), 0.0, tail)
+    for which, (base, end) in enumerate(((-3, start_tail), (-1, tail), (1, tail))):
+        block = jnp.concatenate([taken[base], taken[base + 1], taken[base + 2], end], axis=1)
+        stacked[which * rows : (which + 1) * rows, :] = block.astype(jnp.bfloat16)
+
+    def conv_shard(shard):
+        columns = pl.ds(pl.multiple_of(shard * width, 128), width)
+        summed = jnp.dot(stacked[...], gathered[shard], preferred_element_type=jnp.float32)
+        summed = jnp.maximum(summed, 0.0)
+        total = (
+            summed[0:rows] * depth_weight[0:1, columns]
+            + summed[rows : 2 * rows] * depth_weight[1:2, columns]
+            + summed[2 * rows :] * depth_weight[2:3, columns]
+            + depth_bias[0:1, columns]
+        )
+        subsampled[:, columns] = jnp.maximum(total, 0.0).astype(jnp.bfloat16)
+
+    conv_shard(lane)
+
+    third = []
+    for k in range(count - 1):
+        copies = []
+        for j, (to_group, to_span) in enumerate(chips):
+            second[k][j].wait_recv()
+            copy = send(
+                piece(sources[k], to_group, to_span),
+                (group, sibling, lane),
+                send3.at[k, j],
+                recv3.at[k, j],
+            )
+            copy.start()
+            copies.append(copy)
+        third.append(copies)
+
+    for k in range(count - 1):
+        second[k][3].wait_recv()
+        for copy in third[k]:
+            copy.wait_recv()
+        conv_shard(sources[k])
+
+    chunk = 32
+
+    @pl.loop(0, rows // chunk)
+    def _(step):
+        some = pl.ds(pl.multiple_of(step * chunk, chunk), chunk)
+        values = subsampled[some, :].astype(jnp.float32)
+        centred = values - jnp.sum(values, axis=1, keepdims=True) * (1.0 / channels)
+        variance = jnp.sum(centred * centred, axis=1, keepdims=True) * (1.0 / channels)
+        normed = centred * lax.rsqrt(variance + epsilon)
+        mix_input[some, :] = (normed * mix_gain[...] + mix_shift[...]).astype(jnp.bfloat16)
+        feed_input[some, :] = (normed * feed_gain[...] + feed_shift[...]).astype(jnp.bfloat16)
+
+    def project(source, weight, bias_row, stage, out, sem, load, activation):
+        load.wait()
+        tile = 256
+        whole, rest = tiles_of(stage.shape[1], tile)
+
+        def columns_copy(index, start, size):
+            columns = pl.ds(start, size)
+            return pltpu.make_async_copy(stage.at[:, columns], out.at[:, columns], sem.at[index])
+
+        def one(index, start, size):
+            columns = pl.ds(start, size)
+            summed = jnp.dot(source[...], weight[:, columns], preferred_element_type=jnp.float32)
+            summed = summed + bias_row[0:1, columns]
+            stage[:, columns] = activation(summed).astype(jnp.bfloat16)
+            columns_copy(index, start, size).start()
+
+        @pl.loop(0, whole)
+        def _(index):
+            one(index, pl.multiple_of(index * tile, tile), tile)
+
+        if rest:
+            one(whole, whole * tile, rest)
+
+        def finish():
+            for index in range(whole):
+                columns_copy(index, index * tile, tile).wait()
+            if rest:
+                columns_copy(whole, whole * tile, rest).wait()
+
+        return finish
+
+    finish_heads = project(
+        mix_input, heads_w, heads_bias, heads_stage, heads_out, heads_sem, load_heads, lambda v: v
+    )
+    finish_up = project(
+        feed_input, up_w, up_bias, up_stage, up_out, up_sem, load_up, jax.nn.silu
+    )
+    halo_copy.wait_send()
+    for copy in first:
+        copy.wait_send()
+    for copies in second + third:
+        for copy in copies:
+            copy.wait_send()
+    finish_heads()
+    finish_up()
+
+
+def kernel_device(
+    count,
+    spectrum,
+    conv_weight,
+    conv_bias,
+    depth_weight,
+    depth_bias,
+    mix_gain,
+    mix_shift,
+    feed_gain,
+    feed_shift,
+    heads_weight,
+    heads_bias,
+    up_weight,
+    up_bias,
+):
+    mel_rows, mels = spectrum.shape
+    width = conv_weight.shape[2]
+    channels = depth_weight.shape[1]
+    taps = 3 * mels
+    depth = -(-(taps + 2) // 256) * 256
+    rows = mel_rows // 4
+    heads_cols, up_cols = heads_weight.shape[1], up_weight.shape[1]
+    vmem = pl.BlockSpec(memory_space=pltpu.VMEM)
+    anywhere = pl.BlockSpec(memory_space=pl.ANY)
+    dma = pltpu.SemaphoreType.DMA
+    bf16 = jnp.bfloat16
+    return pl.pallas_call(
+        functools.partial(front_kernel, count, mels),
+        out_shape=(
+            jax.ShapeDtypeStruct((rows, heads_cols), bf16),
+            jax.ShapeDtypeStruct((rows, up_cols), bf16),
+        ),
+        in_specs=[vmem] * 11 + [anywhere] * 2,
+        out_specs=(anywhere, anywhere),
+        scratch_shapes=[
+            pltpu.VMEM((channels, heads_cols), bf16),
+            pltpu.VMEM((channels, up_cols), bf16),
+            pltpu.VMEM((count, depth, width), bf16),
+            pltpu.VMEM((HALO, mels), bf16),
+            pltpu.VMEM((HALO + mel_rows, 128), jnp.float32),
+            pltpu.VMEM((3 * rows, depth), bf16),
+            pltpu.VMEM((rows, channels), bf16),
+            pltpu.VMEM((rows, channels), bf16),
+            pltpu.VMEM((rows, channels), bf16),
+            pltpu.VMEM((rows, heads_cols), bf16),
+            pltpu.VMEM((rows, up_cols), bf16),
+            dma((2,)),
+            dma((2,)),
+            dma((count - 1,)),
+            dma((count - 1,)),
+            dma((count - 1, 4)),
+            dma((count - 1, 4)),
+            dma((count - 1, 3)),
+            dma((count - 1, 3)),
+            dma((-(-heads_cols // 256),)),
+            dma((-(-up_cols // 256),)),
+        ],
+        compiler_params=pltpu.CompilerParams(
+            collective_id=0, has_side_effects=True, vmem_limit_bytes=48 * 2**20
+        ),
+        cost_estimate=pl.CostEstimate(
+            flops=2 * rows * channels * (heads_cols + up_cols + 3 * taps),
+            bytes_accessed=2 * (channels + rows) * (heads_cols + up_cols),
+            transcendentals=rows * up_cols,
+        ),
+        name="front",
+    )(
+        spectrum,
+        conv_weight.reshape(taps, width),
+        conv_bias.reshape(1, -1),
+        depth_weight,
+        depth_bias.reshape(1, -1),
+        mix_gain.reshape(1, -1),
+        mix_shift.reshape(1, -1),
+        feed_gain.reshape(1, -1),
+        feed_shift.reshape(1, -1),
+        heads_bias.reshape(1, -1),
+        up_bias.reshape(1, -1),
+        heads_weight,
+        up_weight,
+    )
 
 
 def solution(mesh):
@@ -101,6 +426,14 @@
         P("tensor"),
     )
     out_specs = (P(("groups", "seq"), "tensor"), P(("groups", "seq"), "tensor"))
+    groups, spans, count = (mesh.shape[name] for name in ("groups", "seq", "tensor"))
+
+    def per_device(*arrays):
+        width = arrays[1].shape[2]
+        if groups == 2 and spans == 4 and count > 1 and width % 128 == 0:
+            return kernel_device(count, *arrays)
+        return plain_device(*arrays)
+
     return jax.shard_map(
         per_device, mesh=mesh, in_specs=in_specs, out_specs=out_specs, check_vma=False
     )

time: 103 us -> 35.3 us (0.34)
  waiting for transfers between devices: 28.8 us -> 0 us
  Pallas kernels: 0 us -> 23.7 us
  local copies, waits for them, and re-layouts: 25 us -> 10.3 us
  blocking collectives: 13.9 us -> 0 us
  between operations: 14.2 us -> 0.66 us
  matrix products: 7.7 us -> 0 us
  starting transfers between devices: 7.47 us -> 0 us
  other arithmetic: 5.43 us -> 0 us
    all_gather x1 -> x0, waiting for transfers between devices: 28.8 us -> none  [per_device(): lax.all_gather(subsampled, 'tensor', axis=0, tiled=True).astype(jnp.float32)]
    pallas_call x0 -> x1, Pallas kernels: none -> 23.7 us  [kernel_device(): pl.pallas_call(functools.partial(front_kernel, count, mels), out_shape=(j...]
    slice x8 -> x0, local copies, waits for them, and re-layouts: 22.6 us -> none  [the longest x1 5.72 us: first_conv(): odd_rows = spectrum[1::2]]
    all_to_all x1 -> x0, blocking collectives: 13.9 us -> none  [per_device(): lax.all_to_all(reduced, 'tensor', split_axis=0, concat_axis=1, tiled=True)]
    dot_general x3 -> x0, matrix products: 7.7 us -> none  [the longest x1 3.31 us: per_device(): jnp.dot(feed_input, up_weight, preferred_element_type=jnp.float32) + up_bias]
    ppermute x2 -> x0, starting transfers between devices: 7.44 us -> none  [passed_along(): lax.ppermute(value, axis, [(source, source + steps) for source in range(i...]
    reshape x0 -> x8, local copies, waits for them, and re-layouts: none -> 5.59 us  [the longest x1 0.7 us: kernel_device(): depth_bias.reshape(1, -1)]
    unnamed x22 -> x7, local copies, waits for them, and re-layouts: 0.87 us -> 4.75 us
  transfers between devices with their start and end apart: 3 -> 0, of which waited for: 1 -> 0; matrix products, arithmetic and copies ran while one was open for 21% -> 0% of each run, Pallas kernels for 0% -> 0%
where the time goes in v1:
time: 35.3 us; the launch traced here: 34.7 us
  Pallas kernels  23.7 us (67%)
  local copies, waits for them, and re-layouts  10.3 us (29%)
  between operations  0.66 us (2%)
    pallas_call x1, Pallas kernels, kernel_device(): pl.pallas_call(functools.partial(front_kernel, count, mels), out_shape=(j...  23.7 us
    unnamed x7, local copies, waits for them, and re-layouts  4.75 us

profile of v1, /device:TPU:0, one launch (start us, length us, event | category | flops | bytes accessed | tf_op | source)
XLA Modules:
  0.0 34.7 jit_solution(17285784183971670733)
XLA Ops:
  0.6 0.7 %reshape.32.conv_bias = f32[1,384]{1,0:T(1,128)S(1)} reshape(f32[384]{0:T(512)} %param.15) | data formatting | bytes 3072 | tf_op jit(solution)/shard_map/reshape | solution.py:398
  1.3 0.7 %reshape.38.heads_bias = f32[1,1152]{1,0:T(1,128)S(1)} reshape(f32[1152]{0:T(1024)} %param.23) | data formatting | bytes 9216 | tf_op jit(solution)/shard_map/reshape | solution.py:405
  2.0 0.7 %reshape.33.depth_bias = f32[1,1536]{1,0:T(1,128)S(1)} reshape(f32[1536]{0:T(1024)} %param.17) | data formatting | bytes 12288 | tf_op jit(solution)/shard_map/reshape | solution.py:400
  2.7 0.7 %reshape.34.mix_gain = f32[1,1536]{1,0:T(1,128)S(1)} reshape(f32[1536]{0:T(1024)} %param.18) | data formatting | bytes 12288 | tf_op jit(solution)/shard_map/reshape | solution.py:401
  3.4 0.7 %reshape.35.mix_shift = f32[1,1536]{1,0:T(1,128)S(1)} reshape(f32[1536]{0:T(1024)} %param.19) | data formatting | bytes 12288 | tf_op jit(solution)/shard_map/reshape | solution.py:402
  4.1 0.7 %reshape.36.feed_gain = f32[1,1536]{1,0:T(1,128)S(1)} reshape(f32[1536]{0:T(1024)} %param.20) | data formatting | bytes 12288 | tf_op jit(solution)/shard_map/reshape | solution.py:403
  4.8 0.7 %reshape.37.feed_shift = f32[1,1536]{1,0:T(1,128)S(1)} reshape(f32[1536]{0:T(1024)} %param.21) | data formatting | bytes 12288 | tf_op jit(solution)/shard_map/reshape | solution.py:404
  5.5 0.7 %reshape.39.up_bias = f32[1,1536]{1,0:T(1,128)S(1)} reshape(f32[1536]{0:T(1024)} %param.25) | data formatting | bytes 12288 | tf_op jit(solution)/shard_map/reshape | solution.py:406
  6.2 1.2 %copy.15.spectrum = bf16[1536,80]{1,0:T(8,128)(2,1)S(1)} copy(bf16[1536,80]{0,1:T(8,128)(2,1)} %param.13) | data formatting | bytes 491520 | tf_op args[0]
  7.4 0.0 copy-start
  7.4 0.9 %copy-done = bf16[3,80,384]{2,1,0:T(8,128)(2,1)S(1)} copy-done((bf16[3,80,384]{2,1,0:T(8,128)(2,1)S(1)}, bf16[3,80,384]{2,1,0:T(8,128)(2,1)}, u32[]{:S(2)}) %copy-start) | copy-done | bytes 184344
  8.3 0.0 copy-start.1
  8.3 0.7 %copy-done.1 = f32[3,1536]{1,0:T(4,128)S(1)} copy-done((f32[3,1536]{1,0:T(4,128)S(1)}, f32[3,1536]{1,0:T(4,128)}, u32[]{:S(2)}) %copy-start.1) | copy-done | bytes 18456
  9.1 23.7 %front.1 = (bf16[384,1152]{1,0:T(8,128)(2,1)S(1)}, bf16[384,1536]{1,0:T(8,128)(2,1)S(1)}) custom-call(bf16[1536,80]{1,0:T(8,128)(2,1)S(1)} %copy.15.spectrum, bf16[240,384]{1,0:T(8,128)(2,1)S(1)} %bitcast.1, f32[1,384]{1,0:T(1,128)S(1)} %reshape.32.conv_bias, f32[3,1536]{1,0:T(4,128)S(1)} %copy-done.1, f32[1,1536]{1,0:T(1,128)S(1)} %reshape.33.depth_bias, ...), custom_call_target="tpu_custom_call" | custom-call | flops 4020240384 | bytes 10321920 | tf_op jit(solution)/shard_map/front/pallas_call | solution.py:355
  32.8 0.9 %copy.18 = bf16[384,1152]{1,0:T(8,128)(2,1)} copy(bf16[384,1152]{1,0:T(8,128)(2,1)S(1)} %get-tuple-element.4) | data formatting | bytes 1769472
  33.7 1.0 %copy.19 = bf16[384,1536]{1,0:T(8,128)(2,1)} copy(bf16[384,1536]{1,0:T(8,128)(2,1)S(1)} %get-tuple-element.5) | data formatting | bytes 2359296
Async XLA Ops:
  7.4 0.9 %copy-start = (bf16[3,80,384]{2,1,0:T(8,128)(2,1)S(1)}, bf16[3,80,384]{2,1,0:T(8,128)(2,1)}, u32[]{:S(2)}) copy-start(bf16[3,80,384]{2,1,0:T(8,128)(2,1)} %param.14) | copy-start | bytes 552964
  8.3 0.7 %copy-start.1 = (f32[3,1536]{1,0:T(4,128)S(1)}, f32[3,1536]{1,0:T(4,128)}, u32[]{:S(2)}) copy-start(f32[3,1536]{1,0:T(4,128)} %depth_weight.1) | copy-start | bytes 55300

commit v2 on v1

--- a/solution.py
+++ b/solution.py
@@ -8,7 +8,7 @@
 from jax.sharding import PartitionSpec as P
 
 epsilon = 1e-05
-HALO = 16
+HALO = 128
 MESH = pl.DeviceIdType.MESH
 
 
@@ -91,9 +91,22 @@
 
 def front_kernel(
     count,
-    mels,
+    spectrum_hbm,
+    conv_hbm,
+    conv_bias_hbm,
+    depth_weight_hbm,
+    depth_bias_hbm,
+    mix_gain_hbm,
+    mix_shift_hbm,
+    feed_gain_hbm,
+    feed_shift_hbm,
+    heads_bias_hbm,
+    up_bias_hbm,
+    heads_hbm,
+    up_hbm,
+    heads_out,
+    up_out,
     spectrum,
-    conv_weight,
     conv_bias,
     depth_weight,
     depth_bias,
@@ -103,10 +116,6 @@
     feed_shift,
     heads_bias,
     up_bias,
-    heads_hbm,
-    up_hbm,
-    heads_out,
-    up_out,
     heads_w,
     up_w,
     gathered,
@@ -132,11 +141,11 @@
     group = lax.axis_index("groups")
     span = lax.axis_index("seq")
     lane = lax.axis_index("tensor")
-    taps, width = conv_weight.shape
+    taps, width = conv_hbm.shape
     depth = gathered.shape[1]
     piece_rows = depth // 8
     rows = subsampled.shape[0]
-    mel_rows = spectrum.shape[0]
+    mels, mel_rows = spectrum.shape
     channels = subsampled.shape[1]
 
     core = lax.rem(span, 2)
@@ -145,8 +154,28 @@
     other = 1 - group
     following = lax.rem(span + 1, 4)
 
-    load_heads = pltpu.make_async_copy(heads_hbm, heads_w, load_sem.at[0])
-    load_up = pltpu.make_async_copy(up_hbm, up_w, load_sem.at[1])
+    def load(index, source, target):
+        return pltpu.make_async_copy(source, target, load_sem.at[index])
+
+    load_conv = load(0, conv_hbm, gathered.at[lane, pl.ds(0, taps), :])
+    load_conv_bias = load(1, conv_bias_hbm, conv_bias.at[0])
+    load_spectrum = load(2, spectrum_hbm, spectrum)
+    small = [
+        (depth_weight_hbm, depth_weight),
+        (depth_bias_hbm, depth_bias.at[0]),
+        (mix_gain_hbm, mix_gain.at[0]),
+        (mix_shift_hbm, mix_shift.at[0]),
+        (feed_gain_hbm, feed_gain.at[0]),
+        (feed_shift_hbm, feed_shift.at[0]),
+        (heads_bias_hbm, heads_bias.at[0]),
+        (up_bias_hbm, up_bias.at[0]),
+    ]
+    small = [load(3 + index, *pair) for index, pair in enumerate(small)]
+    load_heads = load(11, heads_hbm, heads_w)
+    load_up = load(12, up_hbm, up_w)
+    load_conv.start()
+    load_conv_bias.start()
+    load_spectrum.start()
 
     barrier = pltpu.get_barrier_semaphore()
     peers = [(group, span, lax.rem(lane + k, count)) for k in range(1, count)]
@@ -155,13 +184,14 @@
     for peer in peers:
         pl.semaphore_signal(barrier, inc=1, device_id=peer, device_id_type=MESH)
 
-    gathered[lane, 0:taps, :] = conv_weight[...]
+    load_conv_bias.wait()
     bias = conv_bias[...]
     high = bias.astype(jnp.bfloat16).astype(jnp.float32)
     row_id = lax.broadcasted_iota(jnp.int32, (depth - taps, width), 0)
     bias_rows = jnp.where(row_id == 0, high, jnp.where(row_id == 1, bias - high, 0.0))
     gathered[lane, taps:depth, :] = bias_rows.astype(jnp.bfloat16)
 
+    load_conv.wait()
     pl.semaphore_wait(barrier, len(peers))
 
     def piece(shard, owner_group, owner_span):
@@ -190,7 +220,7 @@
         copy.start()
         first.append(copy)
     halo_copy = pltpu.make_async_remote_copy(
-        src_ref=spectrum.at[pl.ds(mel_rows - HALO, HALO), :],
+        src_ref=spectrum_hbm.at[:, pl.ds(mel_rows - HALO, HALO)],
         dst_ref=halo,
         send_sem=halo_sem.at[0],
         recv_sem=halo_sem.at[1],
@@ -198,10 +228,13 @@
         device_id_type=MESH,
     )
     halo_copy.start()
+    for copy in small:
+        copy.start()
     load_heads.start()
     load_up.start()
 
-    frames[HALO : HALO + mel_rows, 0:mels] = spectrum[...].astype(jnp.float32)
+    load_spectrum.wait()
+    frames[HALO : HALO + mel_rows, 0:mels] = spectrum[...].astype(jnp.float32).T
 
     chips = [(group, across), (other, span), (other, across)]
     second = []
@@ -217,7 +250,7 @@
         second.append(copies)
 
     halo_copy.wait_recv()
-    frames[0:HALO, 0:mels] = jnp.where(span == 0, 0.0, halo[...].astype(jnp.float32))
+    frames[0:HALO, 0:mels] = jnp.where(span == 0, 0.0, halo[...].astype(jnp.float32)).T
 
     def tap(offset):
         return frames[pl.ds(HALO + offset, rows, stride=4), :][:, 0:mels]
@@ -243,6 +276,8 @@
         )
         subsampled[:, columns] = jnp.maximum(total, 0.0).astype(jnp.bfloat16)
 
+    for copy in small:
+        copy.wait()
     conv_shard(lane)
 
     third = []
@@ -278,8 +313,8 @@
         mix_input[some, :] = (normed * mix_gain[...] + mix_shift[...]).astype(jnp.bfloat16)
         feed_input[some, :] = (normed * feed_gain[...] + feed_shift[...]).astype(jnp.bfloat16)
 
-    def project(source, weight, bias_row, stage, out, sem, load, activation):
-        load.wait()
+    def project(source, weight, bias_row, stage, out, sem, loaded, activation):
+        loaded.wait()
         tile = 256
         whole, rest = tiles_of(stage.shape[1], tile)
 
@@ -348,23 +383,33 @@
     depth = -(-(taps + 2) // 256) * 256
     rows = mel_rows // 4
     heads_cols, up_cols = heads_weight.shape[1], up_weight.shape[1]
-    vmem = pl.BlockSpec(memory_space=pltpu.VMEM)
+    hbm = pl.BlockSpec(memory_space=pltpu.HBM)
     anywhere = pl.BlockSpec(memory_space=pl.ANY)
     dma = pltpu.SemaphoreType.DMA
     bf16 = jnp.bfloat16
     return pl.pallas_call(
-        functools.partial(front_kernel, count, mels),
+        functools.partial(front_kernel, count),
         out_shape=(
             jax.ShapeDtypeStruct((rows, heads_cols), bf16),
             jax.ShapeDtypeStruct((rows, up_cols), bf16),
         ),
-        in_specs=[vmem] * 11 + [anywhere] * 2,
+        in_specs=[hbm] * 13,
         out_specs=(anywhere, anywhere),
         scratch_shapes=[
+            pltpu.VMEM((mels, mel_rows), bf16),
+            pltpu.VMEM((1, width), jnp.float32),
+            pltpu.VMEM((3, channels), jnp.float32),
+            pltpu.VMEM((1, channels), jnp.float32),
+            pltpu.VMEM((1, channels), jnp.float32),
+            pltpu.VMEM((1, channels), jnp.float32),
+            pltpu.VMEM((1, channels), jnp.float32),
+            pltpu.VMEM((1, channels), jnp.float32),
+            pltpu.VMEM((1, heads_cols), jnp.float32),
+            pltpu.VMEM((1, up_cols), jnp.float32),
             pltpu.VMEM((channels, heads_cols), bf16),
             pltpu.VMEM((channels, up_cols), bf16),
             pltpu.VMEM((count, depth, width), bf16),
-            pltpu.VMEM((HALO, mels), bf16),
+            pltpu.VMEM((mels, HALO), bf16),
             pltpu.VMEM((HALO + mel_rows, 128), jnp.float32),
             pltpu.VMEM((3 * rows, depth), bf16),
             pltpu.VMEM((rows, channels), bf16),
@@ -372,7 +417,7 @@
             pltpu.VMEM((rows, channels), bf16),
             pltpu.VMEM((rows, heads_cols), bf16),
             pltpu.VMEM((rows, up_cols), bf16),
-            dma((2,)),
+            dma((13,)),
             dma((2,)),
             dma((count - 1,)),
             dma((count - 1,)),
@@ -384,7 +429,7 @@
             dma((-(-up_cols // 256),)),
         ],
         compiler_params=pltpu.CompilerParams(
-            collective_id=0, has_side_effects=True, vmem_limit_bytes=48 * 2**20
+            collective_id=0, has_side_effects=True, vmem_limit_bytes=64 * 2**20
         ),
         cost_estimate=pl.CostEstimate(
             flops=2 * rows * channels * (heads_cols + up_cols + 3 * taps),
@@ -393,17 +438,17 @@
         ),
         name="front",
     )(
-        spectrum,
+        spectrum.T,
         conv_weight.reshape(taps, width),
-        conv_bias.reshape(1, -1),
+        conv_bias,
         depth_weight,
-        depth_bias.reshape(1, -1),
-        mix_gain.reshape(1, -1),
-        mix_shift.reshape(1, -1),
-        feed_gain.reshape(1, -1),
-        feed_shift.reshape(1, -1),
-        heads_bias.reshape(1, -1),
-        up_bias.reshape(1, -1),
+        depth_bias,
+        mix_gain,
+        mix_shift,
+        feed_gain,
+        feed_shift,
+        heads_bias,
+        up_bias,
         heads_weight,
         up_weight,
     )

time: 35.3 us -> 29.9 us (0.85); the launches traced: 34.7 us -> 29.7 us
  local copies, waits for them, and re-layouts: 10.3 us -> 4.51 us
  Pallas kernels: 23.7 us -> 24.6 us
    reshape x8 -> x0, local copies, waits for them, and re-layouts: 5.59 us -> none  [the longest x1 0.7 us: kernel_device(): depth_bias.reshape(1, -1)]
    pallas_call x1, Pallas kernels: 23.7 us -> 24.6 us  [kernel_device(): pl.pallas_call(functools.partial(front_kernel, count), out_shape=(jax.Sha...]
    unnamed x7 -> x2, local copies, waits for them, and re-layouts: 4.75 us -> 4.51 us
where the time goes in v2:
time: 29.9 us; the launch traced here: 29.7 us
  Pallas kernels  24.6 us (82%)
  local copies, waits for them, and re-layouts  4.51 us (15%)
  between operations  0.64 us (2%)
    pallas_call x1, Pallas kernels, kernel_device(): pl.pallas_call(functools.partial(front_kernel, count), out_shape=(jax.Sha...  24.6 us
    unnamed x2, local copies, waits for them, and re-layouts  4.51 us

profile of v2, /device:TPU:0, one launch (start us, length us, event | category | flops | bytes accessed | tf_op | source)
XLA Modules:
  0.0 29.7 jit_solution(13440581103571435323)
XLA Ops:
  0.6 24.6 %front.1 = (bf16[384,1152]{1,0:T(8,128)(2,1)}, bf16[384,1536]{1,0:T(8,128)(2,1)}) custom-call(bf16[80,1536]{1,0:T(8,128)(2,1)} %bitcast.2, bf16[240,384]{1,0:T(8,128)(2,1)} %bitcast.3, f32[384]{0:T(512)} %conv_bias_hbm.1, f32[3,1536]{1,0:T(4,128)} %depth_weight_hbm.1, f32[1536]{0:T(1024)} %depth_bias_hbm.1, f32[1536]{0:T(1024)} %mix_gain_hbm.1, ...), custom_call_target="tpu_custom_call" | custom-call | flops 4020240384 | bytes 10321920 | tf_op jit(solution)/shard_map/front/pallas_call | solution.py:390
  25.2 2.1 %copy.17 = bf16[384,1152]{1,0:T(8,128)(2,1)} copy(bf16[384,1152]{1,0:T(8,128)(2,1)} %get-tuple-element.4) | data formatting | bytes 1769472
  27.4 2.4 %copy.18 = bf16[384,1536]{1,0:T(8,128)(2,1)} copy(bf16[384,1536]{1,0:T(8,128)(2,1)} %get-tuple-element.5) | data formatting | bytes 2359296

commit v3 on v2

--- a/solution.py
+++ b/solution.py
@@ -96,37 +96,16 @@
     conv_bias_hbm,
     depth_weight_hbm,
     depth_bias_hbm,
-    mix_gain_hbm,
-    mix_shift_hbm,
-    feed_gain_hbm,
-    feed_shift_hbm,
-    heads_bias_hbm,
-    up_bias_hbm,
-    heads_hbm,
-    up_hbm,
-    heads_out,
-    up_out,
+    subsampled_out,
     spectrum,
     conv_bias,
     depth_weight,
     depth_bias,
-    mix_gain,
-    mix_shift,
-    feed_gain,
-    feed_shift,
-    heads_bias,
-    up_bias,
-    heads_w,
-    up_w,
     gathered,
     halo,
     frames,
     stacked,
     subsampled,
-    mix_input,
-    feed_input,
-    heads_stage,
-    up_stage,
     load_sem,
     halo_sem,
     send1,
@@ -135,8 +114,7 @@
     recv2,
     send3,
     recv3,
-    heads_sem,
-    up_sem,
+    out_sem,
 ):
     group = lax.axis_index("groups")
     span = lax.axis_index("seq")
@@ -146,7 +124,6 @@
     piece_rows = depth // 8
     rows = subsampled.shape[0]
     mels, mel_rows = spectrum.shape
-    channels = subsampled.shape[1]
 
     core = lax.rem(span, 2)
     sibling = span + 1 - 2 * core
@@ -163,16 +140,8 @@
     small = [
         (depth_weight_hbm, depth_weight),
         (depth_bias_hbm, depth_bias.at[0]),
-        (mix_gain_hbm, mix_gain.at[0]),
-        (mix_shift_hbm, mix_shift.at[0]),
-        (feed_gain_hbm, feed_gain.at[0]),
-        (feed_shift_hbm, feed_shift.at[0]),
-        (heads_bias_hbm, heads_bias.at[0]),
-        (up_bias_hbm, up_bias.at[0]),
     ]
     small = [load(3 + index, *pair) for index, pair in enumerate(small)]
-    load_heads = load(11, heads_hbm, heads_w)
-    load_up = load(12, up_hbm, up_w)
     load_conv.start()
     load_conv_bias.start()
     load_spectrum.start()
@@ -230,8 +199,6 @@
     halo_copy.start()
     for copy in small:
         copy.start()
-    load_heads.start()
-    load_up.start()
 
     load_spectrum.wait()
     frames[HALO : HALO + mel_rows, 0:mels] = spectrum[...].astype(jnp.float32).T
@@ -264,7 +231,7 @@
         block = jnp.concatenate([taken[base], taken[base + 1], taken[base + 2], end], axis=1)
         stacked[which * rows : (which + 1) * rows, :] = block.astype(jnp.bfloat16)
 
-    def conv_shard(shard):
+    def conv_shard(index, shard):
         columns = pl.ds(pl.multiple_of(shard * width, 128), width)
         summed = jnp.dot(stacked[...], gathered[shard], preferred_element_type=jnp.float32)
         summed = jnp.maximum(summed, 0.0)
@@ -275,10 +242,15 @@
             + depth_bias[0:1, columns]
         )
         subsampled[:, columns] = jnp.maximum(total, 0.0).astype(jnp.bfloat16)
+        copy = pltpu.make_async_copy(
+            subsampled.at[:, columns], subsampled_out.at[:, columns], out_sem.at[index]
+        )
+        copy.start()
+        return copy
 
     for copy in small:
         copy.wait()
-    conv_shard(lane)
+    stores = [conv_shard(0, lane)]
 
     third = []
     for k in range(count - 1):
@@ -299,11 +271,88 @@
         second[k][3].wait_recv()
         for copy in third[k]:
             copy.wait_recv()
-        conv_shard(sources[k])
-
-    chunk = 32
-
-    @pl.loop(0, rows // chunk)
+        stores.append(conv_shard(k + 1, sources[k]))
+
+    halo_copy.wait_send()
+    for copy in first:
+        copy.wait_send()
+    for copies in second + third:
+        for copy in copies:
+            copy.wait_send()
+    for copy in stores:
+        copy.wait()
+
+
+WEIGHT_PARTS = 4
+
+
+def project_kernel(
+    subsampled_hbm,
+    mix_gain_hbm,
+    mix_shift_hbm,
+    feed_gain_hbm,
+    feed_shift_hbm,
+    heads_bias_hbm,
+    up_bias_hbm,
+    heads_hbm,
+    up_hbm,
+    heads_out,
+    up_out,
+    subsampled,
+    mix_gain,
+    mix_shift,
+    feed_gain,
+    feed_shift,
+    heads_bias,
+    up_bias,
+    heads_w,
+    up_w,
+    mix_input,
+    feed_input,
+    heads_stage,
+    up_stage,
+    load_sem,
+    heads_load,
+    up_load,
+    heads_sem,
+    up_sem,
+):
+    rows, channels = subsampled.shape
+    small = [
+        (subsampled_hbm, subsampled),
+        (mix_gain_hbm, mix_gain.at[0]),
+        (mix_shift_hbm, mix_shift.at[0]),
+        (feed_gain_hbm, feed_gain.at[0]),
+        (feed_shift_hbm, feed_shift.at[0]),
+        (heads_bias_hbm, heads_bias.at[0]),
+        (up_bias_hbm, up_bias.at[0]),
+    ]
+    small = [
+        pltpu.make_async_copy(source, target, load_sem.at[index])
+        for index, (source, target) in enumerate(small)
+    ]
+    for copy in small:
+        copy.start()
+
+    def load_weight(source, target, sem):
+        part = channels // WEIGHT_PARTS
+        copies = []
+        for index in range(WEIGHT_PARTS):
+            some = pl.ds(index * part, part)
+            copies.append(
+                pltpu.make_async_copy(source.at[some, :], target.at[some, :], sem.at[index])
+            )
+            copies[-1].start()
+        return copies
+
+    heads_loads = load_weight(heads_hbm, heads_w, heads_load)
+    up_loads = load_weight(up_hbm, up_w, up_load)
+    for copy in small:
+        copy.wait()
+
+    chunk = 16
+
+    @pl.loop(0, rows // chunk, unroll=4)
     def _(step):
         some = pl.ds(pl.multiple_of(step * chunk, chunk), chunk)
         values = subsampled[some, :].astype(jnp.float32)
@@ -314,7 +363,8 @@
         feed_input[some, :] = (normed * feed_gain[...] + feed_shift[...]).astype(jnp.bfloat16)
 
     def project(source, weight, bias_row, stage, out, sem, loaded, activation):
-        loaded.wait()
+        for copy in loaded:
+            copy.wait()
         tile = 256
         whole, rest = tiles_of(stage.shape[1], tile)
 
@@ -329,9 +379,8 @@
             stage[:, columns] = activation(summed).astype(jnp.bfloat16)
             columns_copy(index, start, size).start()
 
-        @pl.loop(0, whole)
-        def _(index):
-            one(index, pl.multiple_of(index * tile, tile), tile)
+        for index in range(whole):
+            one(index, index * tile, tile)
 
         if rest:
             one(whole, whole * tile, rest)
@@ -345,17 +394,11 @@
         return finish
 
     finish_heads = project(
-        mix_input, heads_w, heads_bias, heads_stage, heads_out, heads_sem, load_heads, lambda v: v
+        mix_input, heads_w, heads_bias, heads_stage, heads_out, heads_sem, heads_loads, lambda v: v
     )
     finish_up = project(
-        feed_input, up_w, up_bias, up_stage, up_out, up_sem, load_up, jax.nn.silu
-    )
-    halo_copy.wait_send()
-    for copy in first:
-        copy.wait_send()
-    for copies in second + third:
-        for copy in copies:
-            copy.wait_send()
+        feed_input, up_w, up_bias, up_stage, up_out, up_sem, up_loads, jax.nn.silu
+    )
     finish_heads()
     finish_up()
 
@@ -387,37 +430,23 @@
     anywhere = pl.BlockSpec(memory_space=pl.ANY)
     dma = pltpu.SemaphoreType.DMA
     bf16 = jnp.bfloat16
-    return pl.pallas_call(
+    f32 = jnp.float32
+    subsampled = pl.pallas_call(
         functools.partial(front_kernel, count),
-        out_shape=(
-            jax.ShapeDtypeStruct((rows, heads_cols), bf16),
-            jax.ShapeDtypeStruct((rows, up_cols), bf16),
-        ),
-        in_specs=[hbm] * 13,
-        out_specs=(anywhere, anywhere),
+        out_shape=jax.ShapeDtypeStruct((rows, channels), bf16),
+        in_specs=[hbm] * 5,
+        out_specs=anywhere,
         scratch_shapes=[
             pltpu.VMEM((mels, mel_rows), bf16),
-            pltpu.VMEM((1, width), jnp.float32),
-            pltpu.VMEM((3, channels), jnp.float32),
-            pltpu.VMEM((1, channels), jnp.float32),
-            pltpu.VMEM((1, channels), jnp.float32),
-            pltpu.VMEM((1, channels), jnp.float32),
-            pltpu.VMEM((1, channels), jnp.float32),
-            pltpu.VMEM((1, channels), jnp.float32),
-            pltpu.VMEM((1, heads_cols), jnp.float32),
-            pltpu.VMEM((1, up_cols), jnp.float32),
-            pltpu.VMEM((channels, heads_cols), bf16),
-            pltpu.VMEM((channels, up_cols), bf16),
+            pltpu.VMEM((1, width), f32),
+            pltpu.VMEM((3, channels), f32),
+            pltpu.VMEM((1, channels), f32),
             pltpu.VMEM((count, depth, width), bf16),
             pltpu.VMEM((mels, HALO), bf16),
-            pltpu.VMEM((HALO + mel_rows, 128), jnp.float32),
+            pltpu.VMEM((HALO + mel_rows, 128), f32),
             pltpu.VMEM((3 * rows, depth), bf16),
             pltpu.VMEM((rows, channels), bf16),
-            pltpu.VMEM((rows, channels), bf16),
-            pltpu.VMEM((rows, channels), bf16),
-            pltpu.VMEM((rows, heads_cols), bf16),
-            pltpu.VMEM((rows, up_cols), bf16),
-            dma((13,)),
+            dma((5,)),
             dma((2,)),
             dma((count - 1,)),
             dma((count - 1,)),
@@ -425,16 +454,15 @@
             dma((count - 1, 4)),
             dma((count - 1, 3)),
             dma((count - 1, 3)),
-            dma((-(-heads_cols // 256),)),
-            dma((-(-up_cols // 256),)),
+            dma((count,)),
         ],
         compiler_params=pltpu.CompilerParams(
             collective_id=0, has_side_effects=True, vmem_limit_bytes=64 * 2**20
         ),
         cost_estimate=pl.CostEstimate(
-            flops=2 * rows * channels * (heads_cols + up_cols + 3 * taps),
-            bytes_accessed=2 * (channels + rows) * (heads_cols + up_cols),
-            transcendentals=rows * up_cols,
+            flops=2 * rows * channels * 3 * taps,
+            bytes_accessed=2 * (mel_rows * mels + taps * width + rows * channels),
+            transcendentals=0,
         ),
         name="front",
     )(
@@ -443,6 +471,44 @@
         conv_bias,
         depth_weight,
         depth_bias,
+    )
+    return pl.pallas_call(
+        project_kernel,
+        out_shape=(
+            jax.ShapeDtypeStruct((rows, heads_cols), bf16),
+            jax.ShapeDtypeStruct((rows, up_cols), bf16),
+        ),
+        in_specs=[hbm] * 9,
+        out_specs=(hbm, hbm),
+        scratch_shapes=[
+            pltpu.VMEM((rows, channels), bf16),
+            pltpu.VMEM((1, channels), f32),
+            pltpu.VMEM((1, channels), f32),
+            pltpu.VMEM((1, channels), f32),
+            pltpu.VMEM((1, channels), f32),
+            pltpu.VMEM((1, heads_cols), f32),
+            pltpu.VMEM((1, up_cols), f32),
+            pltpu.VMEM((channels, heads_cols), bf16),
+            pltpu.VMEM((channels, up_cols), bf16),
+            pltpu.VMEM((rows, channels), bf16),
+            pltpu.VMEM((rows, channels), bf16),
+            pltpu.VMEM((rows, heads_cols), bf16),
+            pltpu.VMEM((rows, up_cols), bf16),
+            dma((7,)),
+            dma((WEIGHT_PARTS,)),
+            dma((WEIGHT_PARTS,)),
+            dma((-(-heads_cols // 256),)),
+            dma((-(-up_cols // 256),)),
+        ],
+        compiler_params=pltpu.CompilerParams(vmem_limit_bytes=64 * 2**20),
+        cost_estimate=pl.CostEstimate(
+            flops=2 * rows * channels * (heads_cols + up_cols),
+            bytes_accessed=2 * (channels + rows) * (heads_cols + up_cols),
+            transcendentals=rows * up_cols,
+        ),
+        name="project",
+    )(
+        subsampled,
         mix_gain,
         mix_shift,
         feed_gain,

time: 29.9 us -> 26.6 us (0.89)
  local copies, waits for them, and re-layouts: 4.51 us -> 0 us
  Pallas kernels: 24.6 us -> 25.8 us
    unnamed x2 -> x0, local copies, waits for them, and re-layouts: 4.51 us -> none
    pallas_call x1 -> x2, Pallas kernels: 24.6 us -> 25.8 us  [the longest x1 16.2 us: kernel_device(): pl.pallas_call(functools.partial(front_kernel, count), out_shape=jax.Shap...]
where the time goes in v3:
time: 26.6 us; the launch traced here: 26.4 us
  Pallas kernels  25.8 us (97%)
  between operations  0.64 us (2%)
    pallas_call x1, Pallas kernels, kernel_device(): pl.pallas_call(functools.partial(front_kernel, count), out_shape=jax.Shap...  16.2 us
    pallas_call x1, Pallas kernels, kernel_device(): pl.pallas_call(project_kernel, out_shape=(jax.ShapeDtypeStruct((rows, hea...  9.51 us

profile of v3, /device:TPU:0, one launch (start us, length us, event | category | flops | bytes accessed | tf_op | source)
XLA Modules:
  0.0 26.4 jit_solution(17349554513033604600)
XLA Ops:
  0.6 16.2 %front.1.subsampled_hbm = bf16[384,1536]{1,0:T(8,128)(2,1)} custom-call(bf16[80,1536]{1,0:T(8,128)(2,1)} %bitcast.2, bf16[240,384]{1,0:T(8,128)(2,1)} %bitcast.3, f32[384]{0:T(512)} %conv_bias_hbm.1, f32[3,1536]{1,0:T(4,128)} %depth_weight_hbm.1, f32[1536]{0:T(1024)} %depth_bias_hbm.1), custom_call_target="tpu_custom_call" | custom-call | flops 849346560 | bytes 1609728 | tf_op jit(solution)/shard_map/front/pallas_call | solution.py:434
  16.9 9.5 %project.1 = (bf16[384,1152]{1,0:T(8,128)(2,1)}, bf16[384,1536]{1,0:T(8,128)(2,1)}) custom-call(bf16[384,1536]{1,0:T(8,128)(2,1)} %front.1.subsampled_hbm, f32[1536]{0:T(1024)} %mix_gain_hbm.1, f32[1536]{0:T(1024)} %mix_shift_hbm.1, f32[1536]{0:T(1024)} %feed_gain_hbm.1, f32[1536]{0:T(1024)} %feed_shift_hbm.1, f32[1152]{0:T(1024)} %heads_bias_hbm.1, ...), custom_call_target="tpu_custom_call" | custom-call | flops 3170893824 | bytes 10321920 | tf_op jit(solution)/shard_map/project/pallas_call | solution.py:475

commit v4 on v3

--- a/solution.py
+++ b/solution.py
@@ -283,72 +283,37 @@
         copy.wait()
 
 
-WEIGHT_PARTS = 4
-
-
 def project_kernel(
-    subsampled_hbm,
-    mix_gain_hbm,
-    mix_shift_hbm,
-    feed_gain_hbm,
-    feed_shift_hbm,
-    heads_bias_hbm,
-    up_bias_hbm,
-    heads_hbm,
-    up_hbm,
+    subsampled,
+    mix_gain_row,
+    mix_shift_row,
+    feed_gain_row,
+    feed_shift_row,
+    heads_bias_row,
+    up_bias_row,
+    heads_w,
+    up_w,
     heads_out,
     up_out,
-    subsampled,
-    mix_gain,
-    mix_shift,
-    feed_gain,
-    feed_shift,
-    heads_bias,
-    up_bias,
-    heads_w,
-    up_w,
     mix_input,
     feed_input,
     heads_stage,
     up_stage,
-    load_sem,
-    heads_load,
-    up_load,
     heads_sem,
     up_sem,
 ):
     rows, channels = subsampled.shape
-    small = [
-        (subsampled_hbm, subsampled),
-        (mix_gain_hbm, mix_gain.at[0]),
-        (mix_shift_hbm, mix_shift.at[0]),
-        (feed_gain_hbm, feed_gain.at[0]),
-        (feed_shift_hbm, feed_shift.at[0]),
-        (heads_bias_hbm, heads_bias.at[0]),
-        (up_bias_hbm, up_bias.at[0]),
-    ]
-    small = [
-        pltpu.make_async_copy(source, target, load_sem.at[index])
-        for index, (source, target) in enumerate(small)
-    ]
-    for copy in small:
-        copy.start()
-
-    def load_weight(source, target, sem):
-        part = channels // WEIGHT_PARTS
-        copies = []
-        for index in range(WEIGHT_PARTS):
-            some = pl.ds(index * part, part)
-            copies.append(
-                pltpu.make_async_copy(source.at[some, :], target.at[some, :], sem.at[index])
-            )
-            copies[-1].start()
-        return copies
-
-    heads_loads = load_weight(heads_hbm, heads_w, heads_load)
-    up_loads = load_weight(up_hbm, up_w, up_load)
-    for copy in small:
-        copy.wait()
+    mix_gain, mix_shift, feed_gain, feed_shift, heads_bias, up_bias = (
+        row[...].reshape(1, -1)
+        for row in (
+            mix_gain_row,
+            mix_shift_row,
+            feed_gain_row,
+            feed_shift_row,
+            heads_bias_row,
+            up_bias_row,
+        )
+    )
 
     chunk = 16
 
@@ -359,12 +324,10 @@
         centred = values - jnp.sum(values, axis=1, keepdims=True) * (1.0 / channels)
         variance = jnp.sum(centred * centred, axis=1, keepdims=True) * (1.0 / channels)
         normed = centred * lax.rsqrt(variance + epsilon)
-        mix_input[some, :] = (normed * mix_gain[...] + mix_shift[...]).astype(jnp.bfloat16)
-        feed_input[some, :] = (normed * feed_gain[...] + feed_shift[...]).astype(jnp.bfloat16)
-
-    def project(source, weight, bias_row, stage, out, sem, loaded, activation):
-        for copy in loaded:
-            copy.wait()
+        mix_input[some, :] = (normed * mix_gain + mix_shift).astype(jnp.bfloat16)
+        feed_input[some, :] = (normed * feed_gain + feed_shift).astype(jnp.bfloat16)
+
+    def project(source, weight, bias_row, stage, out, sem, activation):
         tile = 256
         whole, rest = tiles_of(stage.shape[1], tile)
 
@@ -375,7 +338,7 @@
         def one(index, start, size):
             columns = pl.ds(start, size)
             summed = jnp.dot(source[...], weight[:, columns], preferred_element_type=jnp.float32)
-            summed = summed + bias_row[0:1, columns]
+            summed = summed + bias_row[:, start : start + size]
             stage[:, columns] = activation(summed).astype(jnp.bfloat16)
             columns_copy(index, start, size).start()
 
@@ -394,10 +357,10 @@
         return finish
 
     finish_heads = project(
-        mix_input, heads_w, heads_bias, heads_stage, heads_out, heads_sem, heads_loads, lambda v: v
+        mix_input, heads_w, heads_bias, heads_stage, heads_out, heads_sem, lambda v: v
     )
     finish_up = project(
-        feed_input, up_w, up_bias, up_stage, up_out, up_sem, up_loads, jax.nn.silu
+        feed_input, up_w, up_bias, up_stage, up_out, up_sem, jax.nn.silu
     )
     finish_heads()
     finish_up()
@@ -427,6 +390,7 @@
     rows = mel_rows // 4
     heads_cols, up_cols = heads_weight.shape[1], up_weight.shape[1]
     hbm = pl.BlockSpec(memory_space=pltpu.HBM)
+    vmem = pl.BlockSpec(memory_space=pltpu.VMEM)
     anywhere = pl.BlockSpec(memory_space=pl.ANY)
     dma = pltpu.SemaphoreType.DMA
     bf16 = jnp.bfloat16
@@ -457,20 +421,25 @@
             dma((count,)),
         ],
         compiler_params=pltpu.CompilerParams(
-            collective_id=0, has_side_effects=True, vmem_limit_bytes=64 * 2**20
+            collective_id=0, has_side_effects=True, vmem_limit_bytes=24 * 2**20
         ),
         cost_estimate=pl.CostEstimate(
-            flops=2 * rows * channels * 3 * taps,
-            bytes_accessed=2 * (mel_rows * mels + taps * width + rows * channels),
+            flops=16 * 2 * rows * channels * 3 * taps,
+            bytes_accessed=32 * (mel_rows * mels + taps * width + rows * channels),
             transcendentals=0,
         ),
         name="front",
     )(
-        spectrum.T,
-        conv_weight.reshape(taps, width),
-        conv_bias,
-        depth_weight,
-        depth_bias,
+        *(
+            pltpu.with_memory_space_constraint(array, pltpu.HBM)
+            for array in (
+                spectrum.T,
+                conv_weight.reshape(taps, width),
+                conv_bias,
+                depth_weight,
+                depth_bias,
+            )
+        )
     )
     return pl.pallas_call(
         project_kernel,
@@ -478,29 +447,17 @@
             jax.ShapeDtypeStruct((rows, heads_cols), bf16),
             jax.ShapeDtypeStruct((rows, up_cols), bf16),
         ),
-        in_specs=[hbm] * 9,
+        in_specs=[vmem] * 9,
         out_specs=(hbm, hbm),
         scratch_shapes=[
-            pltpu.VMEM((rows, channels), bf16),
-            pltpu.VMEM((1, channels), f32),
-            pltpu.VMEM((1, channels), f32),
-            pltpu.VMEM((1, channels), f32),
-            pltpu.VMEM((1, channels), f32),
-            pltpu.VMEM((1, heads_cols), f32),
-            pltpu.VMEM((1, up_cols), f32),
-            pltpu.VMEM((channels, heads_cols), bf16),
-            pltpu.VMEM((channels, up_cols), bf16),
             pltpu.VMEM((rows, channels), bf16),
             pltpu.VMEM((rows, channels), bf16),
             pltpu.VMEM((rows, heads_cols), bf16),
             pltpu.VMEM((rows, up_cols), bf16),
-            dma((7,)),
-            dma((WEIGHT_PARTS,)),
-            dma((WEIGHT_PARTS,)),
             dma((-(-heads_cols // 256),)),
             dma((-(-up_cols // 256),)),
         ],
-        compiler_params=pltpu.CompilerParams(vmem_limit_bytes=64 * 2**20),
+        compiler_params=pltpu.CompilerParams(vmem_limit_bytes=24 * 2**20),
         cost_estimate=pl.CostEstimate(
             flops=2 * rows * channels * (heads_cols + up_cols),
             bytes_accessed=2 * (channels + rows) * (heads_cols + up_cols),
@@ -509,12 +466,12 @@
         name="project",
     )(
         subsampled,
-        mix_gain,
-        mix_shift,
-        feed_gain,
-        feed_shift,
-        heads_bias,
-        up_bias,
+        pltpu.with_memory_space_constraint(mix_gain, pltpu.HBM),
+        pltpu.with_memory_space_constraint(mix_shift, pltpu.HBM),
+        pltpu.with_memory_space_constraint(feed_gain, pltpu.HBM),
+        pltpu.with_memory_space_constraint(feed_shift, pltpu.HBM),
+        pltpu.with_memory_space_constraint(heads_bias, pltpu.HBM),
+        pltpu.with_memory_space_constraint(up_bias, pltpu.HBM),
         heads_weight,
         up_weight,
     )

time: 26.6 us -> 23.4 us (0.88)
  Pallas kernels: 25.8 us -> 22.6 us
    pallas_call x1, Pallas kernels: 9.51 us -> 6.86 us  [kernel_device(): pl.pallas_call(project_kernel, out_shape=(jax.ShapeDtypeStruct((rows, hea...]
    pallas_call x1, Pallas kernels: 16.2 us -> 15.7 us  [kernel_device(): pl.pallas_call(functools.partial(front_kernel, count), out_shape=jax.Shap...]
where the time goes in v4:
time: 23.4 us; the launch traced here: 23.2 us
  Pallas kernels  22.6 us (97%)
  between operations  0.67 us (3%)
    pallas_call x1, Pallas kernels, kernel_device(): pl.pallas_call(functools.partial(front_kernel, count), out_shape=jax.Shap...  15.7 us
    pallas_call x1, Pallas kernels, kernel_device(): pl.pallas_call(project_kernel, out_shape=(jax.ShapeDtypeStruct((rows, hea...  6.86 us

profile of v4, /device:TPU:0, one launch (start us, length us, event | category | flops | bytes accessed | tf_op | source)
XLA Modules:
  0.0 23.2 jit_solution(1026931667164746684)
XLA Ops:
  0.6 0.0 copy-start
  0.6 0.0 copy-start.1
  0.7 15.7 %front.1.subsampled = bf16[384,1536]{1,0:T(8,128)(2,1)S(1)} custom-call(bf16[80,1536]{1,0:T(8,128)(2,1)} %bitcast.2, bf16[240,384]{1,0:T(8,128)(2,1)} %bitcast.3, f32[384]{0:T(512)} %conv_bias_hbm.1, f32[3,1536]{1,0:T(4,128)} %depth_weight_hbm.1, f32[1536]{0:T(1024)} %depth_bias_hbm.1), custom_call_target="tpu_custom_call" | custom-call | flops 13589544960 | bytes 25755648 | tf_op jit(solution)/shard_map/front/pallas_call | solution.py:398
  16.4 0.0 copy-done
  16.4 0.0 copy-done.1
  16.4 6.9 %project.1 = (bf16[384,1152]{1,0:T(8,128)(2,1)}, bf16[384,1536]{1,0:T(8,128)(2,1)}) custom-call(bf16[384,1536]{1,0:T(8,128)(2,1)S(1)} %front.1.subsampled, f32[1536]{0:T(1024)} %mix_gain_row.1, f32[1536]{0:T(1024)} %mix_shift_row.1, f32[1536]{0:T(1024)} %feed_gain_row.1, f32[1536]{0:T(1024)} %feed_shift_row.1, f32[1152]{0:T(1024)} %heads_bias_row.1, ...), custom_call_target="tpu_custom_call" | custom-call | flops 3170893824 | bytes 10321920 | tf_op jit(solution)/shard_map/project/pallas_call | solution.py:444
Async XLA Ops:
  0.6 15.7 %copy-start = (bf16[1536,1536]{1,0:T(8,128)(2,1)S(1)}, bf16[1536,1536]{1,0:T(8,128)(2,1)}, u32[]{:S(2)}) copy-start(bf16[1536,1536]{1,0:T(8,128)(2,1)} %up_w.1) | copy-start | bytes 14155780
  0.6 15.7 %copy-start.1 = (bf16[1536,1152]{1,0:T(8,128)(2,1)S(1)}, bf16[1536,1152]{1,0:T(8,128)(2,1)}, u32[]{:S(2)}) copy-start(bf16[1536,1152]{1,0:T(8,128)(2,1)} %heads_w.1) | copy-start | bytes 10616836

commit v5 on v4

--- a/solution.py
+++ b/solution.py
@@ -145,6 +145,8 @@
     load_conv.start()
     load_conv_bias.start()
     load_spectrum.start()
+    for copy in small:
+        copy.start()
 
     barrier = pltpu.get_barrier_semaphore()
     peers = [(group, span, lax.rem(lane + k, count)) for k in range(1, count)]
@@ -160,6 +162,23 @@
     bias_rows = jnp.where(row_id == 0, high, jnp.where(row_id == 1, bias - high, 0.0))
     gathered[lane, taps:depth, :] = bias_rows.astype(jnp.bfloat16)
 
+    def stack(some):
+        taken = {
+            offset: frames[pl.ds(HALO + offset, some, stride=4), :][:, 0:mels]
+            for offset in range(-3, 4)
+        }
+        tail_id = lax.broadcasted_iota(jnp.int32, (some, depth - taps), 1)
+        tail = jnp.where(tail_id < 2, 1.0, 0.0)
+        row_zero = lax.broadcasted_iota(jnp.int32, (some, depth - taps), 0) == 0
+        start_tail = jnp.where(row_zero & (span == 0), 0.0, tail)
+        for which, (base, end) in enumerate(((-3, start_tail), (-1, tail), (1, tail))):
+            block = jnp.concatenate([taken[base], taken[base + 1], taken[base + 2], end], axis=1)
+            stacked[which * rows : which * rows + some, :] = block.astype(jnp.bfloat16)
+
+    load_spectrum.wait()
+    frames[0:HALO, :] = jnp.zeros((HALO, frames.shape[1]), jnp.float32)
+    frames[HALO : HALO + mel_rows, 0:mels] = spectrum[...].astype(jnp.float32).T
+    stack(rows)
     load_conv.wait()
     pl.semaphore_wait(barrier, len(peers))
 
@@ -189,7 +208,7 @@
         copy.start()
         first.append(copy)
     halo_copy = pltpu.make_async_remote_copy(
-        src_ref=spectrum_hbm.at[:, pl.ds(mel_rows - HALO, HALO)],
+        src_ref=spectrum.at[:, pl.ds(mel_rows - HALO, HALO)],
         dst_ref=halo,
         send_sem=halo_sem.at[0],
         recv_sem=halo_sem.at[1],
@@ -197,11 +216,7 @@
         device_id_type=MESH,
     )
     halo_copy.start()
-    for copy in small:
-        copy.start()
-
-    load_spectrum.wait()
-    frames[HALO : HALO + mel_rows, 0:mels] = spectrum[...].astype(jnp.float32).T
+
 
     chips = [(group, across), (other, span), (other, across)]
     second = []
@@ -218,18 +233,7 @@
 
     halo_copy.wait_recv()
     frames[0:HALO, 0:mels] = jnp.where(span == 0, 0.0, halo[...].astype(jnp.float32)).T
-
-    def tap(offset):
-        return frames[pl.ds(HALO + offset, rows, stride=4), :][:, 0:mels]
-
-    taken = {offset: tap(offset) for offset in range(-3, 4)}
-    tail_id = lax.broadcasted_iota(jnp.int32, (rows, depth - taps), 1)
-    tail = jnp.where(tail_id < 2, 1.0, 0.0)
-    row_zero = lax.broadcasted_iota(jnp.int32, (rows, depth - taps), 0) == 0
-    start_tail = jnp.where(row_zero & (span == 0), 0.0, tail)
-    for which, (base, end) in enumerate(((-3, start_tail), (-1, tail), (1, tail))):
-        block = jnp.concatenate([taken[base], taken[base + 1], taken[base + 2], end], axis=1)
-        stacked[which * rows : (which + 1) * rows, :] = block.astype(jnp.bfloat16)
+    stack(32)
 
     def conv_shard(index, shard):
         columns = pl.ds(pl.multiple_of(shard * width, 128), width)
@@ -252,6 +256,12 @@
         copy.wait()
     stores = [conv_shard(0, lane)]
 
+    def finish_shard(k):
+        second[k][3].wait_recv()
+        for copy in third[k]:
+            copy.wait_recv()
+        stores.append(conv_shard(k + 1, sources[k]))
+
     third = []
     for k in range(count - 1):
         copies = []
@@ -266,13 +276,9 @@
             copy.start()
             copies.append(copy)
         third.append(copies)
-
-    for k in range(count - 1):
-        second[k][3].wait_recv()
-        for copy in third[k]:
-            copy.wait_recv()
-        stores.append(conv_shard(k + 1, sources[k]))
-
+        if k:
+            finish_shard(k - 1)
+    finish_shard(count - 2)
     halo_copy.wait_send()
     for copy in first:
         copy.wait_send()

time: 23.4 us -> 24.5 us (1.047)
  Pallas kernels: 22.6 us -> 23.6 us
    pallas_call x1, Pallas kernels: 15.7 us -> 16.8 us  [kernel_device(): pl.pallas_call(functools.partial(front_kernel, count), out_shape=jax.Shap...]
where the time goes in v5:
time: 24.5 us; the launch traced here: 24.3 us
  Pallas kernels  23.6 us (96%)
  between operations  0.67 us (3%)
    pallas_call x1, Pallas kernels, kernel_device(): pl.pallas_call(functools.partial(front_kernel, count), out_shape=jax.Shap...  16.8 us
    pallas_call x1, Pallas kernels, kernel_device(): pl.pallas_call(project_kernel, out_shape=(jax.ShapeDtypeStruct((rows, hea...  6.86 us

profile of v5, /device:TPU:0, one launch (start us, length us, event | category | flops | bytes accessed | tf_op | source)
XLA Modules:
  0.0 24.3 jit_solution(12704608633001889390)
XLA Ops:
  0.6 0.0 copy-start
  0.6 0.0 copy-start.1
  0.7 16.8 %front.1.subsampled = bf16[384,1536]{1,0:T(8,128)(2,1)S(1)} custom-call(bf16[80,1536]{1,0:T(8,128)(2,1)} %bitcast.2, bf16[240,384]{1,0:T(8,128)(2,1)} %bitcast.3, f32[384]{0:T(512)} %conv_bias_hbm.1, f32[3,1536]{1,0:T(4,128)} %depth_weight_hbm.1, f32[1536]{0:T(1024)} %depth_bias_hbm.1), custom_call_target="tpu_custom_call" | custom-call | flops 13589544960 | bytes 25755648 | tf_op jit(solution)/shard_map/front/pallas_call | solution.py:404
  17.4 0.0 copy-done
  17.4 0.0 copy-done.1
  17.4 6.9 %project.1 = (bf16[384,1152]{1,0:T(8,128)(2,1)}, bf16[384,1536]{1,0:T(8,128)(2,1)}) custom-call(bf16[384,1536]{1,0:T(8,128)(2,1)S(1)} %front.1.subsampled, f32[1536]{0:T(1024)} %mix_gain_row.1, f32[1536]{0:T(1024)} %mix_shift_row.1, f32[1536]{0:T(1024)} %feed_gain_row.1, f32[1536]{0:T(1024)} %feed_shift_row.1, f32[1152]{0:T(1024)} %heads_bias_row.1, ...), custom_call_target="tpu_custom_call" | custom-call | flops 3170893824 | bytes 10321920 | tf_op jit(solution)/shard_map/project/pallas_call | solution.py:450
Async XLA Ops:
  0.6 16.8 %copy-start = (bf16[1536,1536]{1,0:T(8,128)(2,1)S(1)}, bf16[1536,1536]{1,0:T(8,128)(2,1)}, u32[]{:S(2)}) copy-start(bf16[1536,1536]{1,0:T(8,128)(2,1)} %up_w.1) | copy-start | bytes 14155780
  0.6 16.8 %copy-start.1 = (bf16[1536,1152]{1,0:T(8,128)(2,1)S(1)}, bf16[1536,1152]{1,0:T(8,128)(2,1)}, u32[]{:S(2)}) copy-start(bf16[1536,1152]{1,0:T(8,128)(2,1)} %heads_w.1) | copy-start | bytes 10616836

commit v6 on v4

--- a/solution.py
+++ b/solution.py
@@ -200,8 +200,6 @@
     for copy in small:
         copy.start()
 
-    load_spectrum.wait()
-    frames[HALO : HALO + mel_rows, 0:mels] = spectrum[...].astype(jnp.float32).T
 
     chips = [(group, across), (other, span), (other, across)]
     second = []
@@ -216,6 +214,8 @@
             copy.start()
         second.append(copies)
 
+    load_spectrum.wait()
+    frames[HALO : HALO + mel_rows, 0:mels] = spectrum[...].astype(jnp.float32).T
     halo_copy.wait_recv()
     frames[0:HALO, 0:mels] = jnp.where(span == 0, 0.0, halo[...].astype(jnp.float32)).T
 
@@ -252,6 +252,12 @@
         copy.wait()
     stores = [conv_shard(0, lane)]
 
+    def finish_shard(k):
+        second[k][3].wait_recv()
+        for copy in third[k]:
+            copy.wait_recv()
+        stores.append(conv_shard(k + 1, sources[k]))
+
     third = []
     for k in range(count - 1):
         copies = []
@@ -266,13 +272,9 @@
             copy.start()
             copies.append(copy)
         third.append(copies)
-
-    for k in range(count - 1):
-        second[k][3].wait_recv()
-        for copy in third[k]:
-            copy.wait_recv()
-        stores.append(conv_shard(k + 1, sources[k]))
-
+        if k:
+            finish_shard(k - 1)
+    finish_shard(count - 2)
     halo_copy.wait_send()
     for copy in first:
         copy.wait_send()

time: 23.4 us -> 23.8 us (1.017)
  Pallas kernels: 22.6 us -> 23 us
    pallas_call x1, Pallas kernels: 15.7 us -> 16.1 us  [kernel_device(): pl.pallas_call(functools.partial(front_kernel, count), out_shape=jax.Shap...]
where the time goes in v6:
time: 23.8 us; the launch traced here: 23.6 us
  Pallas kernels  23 us (97%)
  between operations  0.67 us (3%)
    pallas_call x1, Pallas kernels, kernel_device(): pl.pallas_call(functools.partial(front_kernel, count), out_shape=jax.Shap...  16.1 us
    pallas_call x1, Pallas kernels, kernel_device(): pl.pallas_call(project_kernel, out_shape=(jax.ShapeDtypeStruct((rows, hea...  6.86 us

profile of v6, /device:TPU:0, one launch (start us, length us, event | category | flops | bytes accessed | tf_op | source)
XLA Modules:
  0.0 23.6 jit_solution(10353087209997228073)
XLA Ops:
  0.6 0.0 copy-start
  0.6 0.0 copy-start.1
  0.7 16.1 %front.1.subsampled = bf16[384,1536]{1,0:T(8,128)(2,1)S(1)} custom-call(bf16[80,1536]{1,0:T(8,128)(2,1)} %bitcast.2, bf16[240,384]{1,0:T(8,128)(2,1)} %bitcast.3, f32[384]{0:T(512)} %conv_bias_hbm.1, f32[3,1536]{1,0:T(4,128)} %depth_weight_hbm.1, f32[1536]{0:T(1024)} %depth_bias_hbm.1), custom_call_target="tpu_custom_call" | custom-call | flops 13589544960 | bytes 25755648 | tf_op jit(solution)/shard_map/front/pallas_call | solution.py:400
  16.8 0.0 copy-done
  16.8 0.0 copy-done.1
  16.8 6.9 %project.1 = (bf16[384,1152]{1,0:T(8,128)(2,1)}, bf16[384,1536]{1,0:T(8,128)(2,1)}) custom-call(bf16[384,1536]{1,0:T(8,128)(2,1)S(1)} %front.1.subsampled, f32[1536]{0:T(1024)} %mix_gain_row.1, f32[1536]{0:T(1024)} %mix_shift_row.1, f32[1536]{0:T(1024)} %feed_gain_row.1, f32[1536]{0:T(1024)} %feed_shift_row.1, f32[1152]{0:T(1024)} %heads_bias_row.1, ...), custom_call_target="tpu_custom_call" | custom-call | flops 3170893824 | bytes 10321920 | tf_op jit(solution)/shard_map/project/pallas_call | solution.py:446
Async XLA Ops:
  0.6 16.1 %copy-start = (bf16[1536,1536]{1,0:T(8,128)(2,1)S(1)}, bf16[1536,1536]{1,0:T(8,128)(2,1)}, u32[]{:S(2)}) copy-start(bf16[1536,1536]{1,0:T(8,128)(2,1)} %up_w.1) | copy-start | bytes 14155780
  0.6 16.1 %copy-start.1 = (bf16[1536,1152]{1,0:T(8,128)(2,1)S(1)}, bf16[1536,1152]{1,0:T(8,128)(2,1)}, u32[]{:S(2)}) copy-start(bf16[1536,1152]{1,0:T(8,128)(2,1)} %heads_w.1) | copy-start | bytes 10616836
